TPU v7x, 256 devices: a whole 4x4x8 slice. The times are simulated.
256 devices in a mesh: energy: 16 (over x_lo, y, core), tile: 16 (over x_hi, z).
Axes of the slice: x: 4 (x_hi: 2, x_lo: 2; x = x_hi * 2 + x_lo), y: 4, z: 8, core: 2. Of those that a mesh axis runs over, the one named last changes fastest.
Arguments:
- lesser: float32 [2, 512, 16, 4096], P(None, 'energy', 'tile'), may hold values from -6 to 6
- greater: float32 [2, 512, 16, 4096], P(None, 'energy', 'tile'), may hold values from -6 to 6
Outputs:
- polarization: float32 [2, 512, 16, 4096], P(None, 'energy', 'tile')
All inputs are finite; a program needn't handle non-finite values.
Results may differ from a plain program's by a relative error of at most 0.000098.
Values sent between devices are 32-bit elements; how exact they have to be, the bound alone decides.
A program may use at most 64 MiB of HBM per device.

v0:
```python
import functools
import math

import jax
import jax.numpy as jnp
import ml_dtypes
import numpy as np
from jax import lax
from jax.experimental import pallas as pl
from jax.experimental.pallas import tpu as pltpu
from jax.sharding import PartitionSpec as P

MESH = pl.DeviceIdType.MESH
BF = jnp.bfloat16
F32 = jnp.float32


def tables(energies, lanes):
    length = 2 * energies
    quarter = length // 4
    n = np.arange(quarter)
    angle = 2.0 * np.pi * (np.outer(n, n) % quarter) / quarter
    cos, sin = np.cos(angle), np.sin(angle)
    full = np.block([[cos, sin], [-sin, cos]]).astype(np.float32)
    high = full.astype(ml_dtypes.bfloat16)
    low = (full - high.astype(np.float32)).astype(ml_dtypes.bfloat16)
    rows = []
    for q in (1, 2, 3):
        turn = 2.0 * np.pi * ((n * q) % length) / length
        rows.append(np.stack([np.cos(turn), -np.sin(turn)]))
    twiddle = np.stack(rows).astype(np.float32)
    twiddle = np.ascontiguousarray(np.broadcast_to(twiddle[..., None], twiddle.shape + (lanes,)))
    return np.stack([high, low]), twiddle


def split(x):
    high = x.astype(BF)
    return high, (x - high.astype(F32)).astype(BF)


def body(
    n_energy, side, lesser, greater, dft_hbm, tw_hbm, out,
    g_in, stage, turned, mirror_out, l_buf, g_buf, p_buf, dft, tw, y_hi, y_lo, spec, v_hi, v_lo, back,
    in_sem, own_sem, l_send, g_send, p_send, l_recv, g_recv, p_recv,
):
    e = lax.axis_index("energy")
    t = lax.axis_index("tile")
    t2 = (t % side) * side + t // side
    off_diagonal = t2 != t
    local = g_in.shape[1]
    energies = n_energy * local
    half = energies // 2

    load_g = pltpu.make_async_copy(greater, g_in, in_sem.at[0])
    load_g.start()
    load_dft = pltpu.make_async_copy(dft_hbm, dft, in_sem.at[1])
    load_tw = pltpu.make_async_copy(tw_hbm, tw, in_sem.at[2])

    barrier = pltpu.get_barrier_semaphore()

    @pl.loop(1, n_energy)
    def _(m):
        pl.semaphore_signal(barrier, inc=1, device_id=((e + m) % n_energy, t), device_id_type=MESH)

    @pl.when(off_diagonal)
    def _():
        @pl.loop(0, n_energy)
        def _(m):
            pl.semaphore_signal(barrier, inc=1, device_id=((e + m) % n_energy, t2), device_id_type=MESH)

        pl.semaphore_wait(barrier, 2 * n_energy - 1)

    @pl.when(jnp.logical_not(off_diagonal))
    def _():
        pl.semaphore_wait(barrier, n_energy - 1)

    def l_copy(h, to, frm):
        return pltpu.make_async_remote_copy(
            src_ref=lesser.at[:, :, 2 * to + h],
            dst_ref=l_buf.at[h, :, pl.ds(pl.multiple_of(frm * local, local), local)],
            send_sem=l_send.at[h, to],
            recv_sem=l_recv.at[h, frm],
            device_id=(to, t),
            device_id_type=MESH,
        )

    def g_copy(h, to, frm):
        return pltpu.make_async_remote_copy(
            src_ref=mirror_out.at[:, :, 2 * to + h],
            dst_ref=g_buf.at[h, :, pl.ds(pl.multiple_of(frm * local, local), local)],
            send_sem=g_send.at[h, to],
            recv_sem=g_recv.at[h, frm],
            device_id=(to, t2),
            device_id_type=MESH,
        )

    def p_copy(h, to, frm):
        return pltpu.make_async_remote_copy(
            src_ref=p_buf.at[h, :, pl.ds(pl.multiple_of(to * local, local), local)],
            dst_ref=out.at[:, :, 2 * frm + h],
            send_sem=p_send.at[h, to],
            recv_sem=p_recv.at[h, frm],
            device_id=(to, t),
            device_id_type=MESH,
        )

    def l_own(h):
        return pltpu.make_async_copy(
            lesser.at[:, :, 2 * e + h], l_buf.at[h, :, pl.ds(pl.multiple_of(e * local, local), local)], l_recv.at[h, e]
        )

    def g_own(h):
        return pltpu.make_async_copy(
            mirror_out.at[:, :, 2 * e + h], g_buf.at[h, :, pl.ds(pl.multiple_of(e * local, local), local)], g_recv.at[h, e]
        )

    def p_own(h):
        return pltpu.make_async_copy(
            p_buf.at[h, :, pl.ds(pl.multiple_of(e * local, local), local)], out.at[:, :, 2 * e + h], p_recv.at[h, e]
        )

    def send_l(h):
        @pl.loop(1, n_energy)
        def _(m):
            l_copy(h, (e + m) % n_energy, e).start()

        l_own(h).start()

    def send_g(h):
        @pl.loop(1, n_energy)
        def _(m):
            g_copy(h, (e + m) % n_energy, e).start()

        @pl.when(off_diagonal)
        def _():
            g_copy(h, e, e).start()

        @pl.when(jnp.logical_not(off_diagonal))
        def _():
            g_own(h).start()

    send_l(0)
    load_g.wait()

    low_lanes = lax.broadcasted_iota(jnp.int32, (32, 128), 1) < 64

    @pl.loop(0, 2 * (local // 4))
    def _(step):
        p = step // (local // 4)
        e0 = (step % (local // 4)) * 4
        for q in range(2):
            one = g_in[p, e0 + 2 * q]
            two = g_in[p, e0 + 2 * q + 1]
            stage[pl.ds(64 * q, 32, stride=2), :] = jnp.where(low_lanes, one, pltpu.roll(two, 64, 1))
            stage[pl.ds(64 * q + 1, 32, stride=2), :] = jnp.where(low_lanes, pltpu.roll(one, 64, 1), two)
        turned[...] = stage[...].T
        for w in range(2):
            even = turned[pl.ds(64 * w, 32, stride=2), :]
            odd = turned[pl.ds(64 * w + 1, 32, stride=2), :]
            mirror_out[p, e0 + w] = jnp.where(low_lanes, even, pltpu.roll(odd, 64, 1))
            mirror_out[p, e0 + 2 + w] = jnp.where(low_lanes, pltpu.roll(even, 64, 1), odd)

    send_g(0)
    send_l(1)
    send_g(1)
    load_dft.start()
    load_tw.start()
    load_dft.wait()
    load_tw.wait()

    factor = 1.0 / (2 * energies * math.sqrt(energies))

    def put(column, re, im):
        hi, lo = split(re)
        y_hi[:half, column : column + 128] = hi
        y_lo[:half, column : column + 128] = lo
        hi, lo = split(im)
        y_hi[half:, column : column + 128] = hi
        y_lo[half:, column : column + 128] = lo

    def front(buf, h, base, sign):
        re0, re1 = buf[h, 0, :half], buf[h, 0, half:]
        im0, im1 = sign * buf[h, 1, :half], sign * buf[h, 1, half:]
        put(base, re0 + re1, im0 + im1)
        for q, re, im in (
            (1, re0 + im1, im0 - re1),
            (2, re0 - re1, im0 - im1),
            (3, re0 - im1, im0 + re1),
        ):
            c, s = tw[q - 1, 0], tw[q - 1, 1]
            put(base + 128 * q, re * c - im * s, re * s + im * c)

    def dots(hi, lo, columns):
        dot = functools.partial(jnp.dot, preferred_element_type=F32)
        return (
            dot(dft[0], hi[:, columns]) + dot(dft[0], lo[:, columns]) + dot(dft[1], hi[:, columns])
        )

    @pl.loop(0, 2)
    def _(h):
        @pl.loop(1, n_energy)
        def _(m):
            l_copy(h, e, (e + n_energy - m) % n_energy).wait_recv()

        l_own(h).wait()

        @pl.loop(0, n_energy)
        def _(m):
            frm = (e + n_energy - m) % n_energy
            pltpu.make_async_copy(
                mirror_out.at[:, :, 0], g_buf.at[h, :, pl.ds(pl.multiple_of(frm * local, local), local)], g_recv.at[h, frm]
            ).wait()

        front(l_buf, h, 0, 1.0)
        front(g_buf, h, 512, -1.0)
        for c in range(4):
            columns = slice(256 * c, 256 * c + 256)
            spec[:, columns] = dots(y_hi, y_lo, columns)
        for c in range(4):
            one, two = slice(128 * c, 128 * c + 128), slice(512 + 128 * c, 640 + 128 * c)
            ar, ai = spec[:half, one], spec[half:, one]
            br, bi = spec[:half, two], spec[half:, two]
            hi, lo = split(ar * br + ai * bi)
            v_hi[:half, one] = hi
            v_lo[:half, one] = lo
            hi, lo = split(ar * bi - ai * br)
            v_hi[half:, one] = hi
            v_lo[half:, one] = lo
        for c in range(2):
            columns = slice(256 * c, 256 * c + 256)
            back[:, columns] = dots(v_hi, v_lo, columns)
        terms = [(back[:half, :128], back[half:, :128])]
        for q in (1, 2, 3):
            re, im = back[:half, 128 * q : 128 * q + 128], back[half:, 128 * q : 128 * q + 128]
            c, s = tw[q - 1, 0], tw[q - 1, 1]
            terms.append((re * c - im * s, re * s + im * c))
        (r0, i0), (r1, i1), (r2, i2), (r3, i3) = terms
        p_buf[h, 0, :half] = (i0 + i1 + i2 + i3) * -factor
        p_buf[h, 1, :half] = (r0 + r1 + r2 + r3) * -factor
        p_buf[h, 0, half:] = (i0 - r1 - i2 + r3) * -factor
        p_buf[h, 1, half:] = (r0 + i1 - r2 - i3) * -factor

        @pl.loop(1, n_energy)
        def _(m):
            p_copy(h, (e + m) % n_energy, e).start()

        p_own(h).start()

    @pl.loop(0, 2)
    def _(h):
        @pl.loop(1, n_energy)
        def _(m):
            to = (e + m) % n_energy
            l_copy(h, to, e).wait_send()
            g_copy(h, to, e).wait_send()
            p_copy(h, to, e).wait_send()
            p_copy(h, e, to).wait_recv()

        p_own(h).wait()

        @pl.when(off_diagonal)
        def _():
            g_copy(h, e, e).wait_send()


def on_device(lesser, greater):
    n_energy = lax.axis_size("energy")
    side = math.isqrt(lax.axis_size("tile"))
    local, cells = lesser.shape[1], lesser.shape[3]
    rows = cells // 128
    energies = n_energy * local
    dft, twiddle = tables(energies, 128)
    any_space = pl.BlockSpec(memory_space=pltpu.HBM)
    half = energies // 2
    out = pl.pallas_call(
        functools.partial(body, n_energy, side),
        out_shape=jax.ShapeDtypeStruct((2, local, rows, 128), F32),
        in_specs=[any_space] * 4,
        out_specs=any_space,
        scratch_shapes=[
            pltpu.VMEM((2, local, rows, 128), F32),
            pltpu.VMEM((128, 128), F32),
            pltpu.VMEM((128, 128), F32),
            pltpu.VMEM((2, local, rows, 128), F32),
            pltpu.VMEM((2, 2, energies, 128), F32),
            pltpu.VMEM((2, 2, energies, 128), F32),
            pltpu.VMEM((2, 2, energies, 128), F32),
            pltpu.VMEM((2, energies, energies), BF),
            pltpu.VMEM((3, 2, half, 128), F32),
            pltpu.VMEM((energies, 1024), BF),
            pltpu.VMEM((energies, 1024), BF),
            pltpu.VMEM((energies, 1024), F32),
            pltpu.VMEM((energies, 512), BF),
            pltpu.VMEM((energies, 512), BF),
            pltpu.VMEM((energies, 512), F32),
            pltpu.SemaphoreType.DMA((3,)),
            pltpu.SemaphoreType.DMA((2,)),
        ]
        + [pltpu.SemaphoreType.DMA((2, n_energy))] * 6,
        compiler_params=pltpu.CompilerParams(
            collective_id=0, has_side_effects=True, vmem_limit_bytes=40 * 2**20
        ),
        name="correlate",
    )(
        lesser.reshape(2, local, rows, 128),
        greater.reshape(2, local, rows, 128),
        jnp.asarray(dft),
        jnp.asarray(twiddle),
    )
    return out.reshape(2, local, 1, cells)


def solution(mesh):
    return jax.shard_map(
        on_device,
        mesh=mesh,
        in_specs=(P(None, "energy", "tile", None), P(None, "energy", "tile", None)),
        out_specs=P(None, "energy", "tile", None),
        check_vma=False,
    )
```

profile of v0, /device:TPU:97, one launch (start us, length us, event | category | flops | bytes accessed | tf_op | source)
XLA Modules:
  0.0 80.8 jit_solution(8259487791743782565)
XLA Ops:
  0.0 0.0 copy-start
  0.0 1.2 %copy-done = f32[2,32,1,4096]{3,2,1,0:T(1,128)S(1)} copy-done((f32[2,32,1,4096]{3,2,1,0:T(1,128)S(1)}, f32[2,32,1,4096]{3,2,1,0:T(1,128)}, u32[]{:S(2)}) %copy-start) | copy-done | bytes 1048600
  1.2 0.0 copy-start.1
  1.2 1.2 %copy-done.1 = f32[2,32,1,4096]{3,2,1,0:T(1,128)S(1)} copy-done((f32[2,32,1,4096]{3,2,1,0:T(1,128)S(1)}, f32[2,32,1,4096]{3,2,1,0:T(1,128)}, u32[]{:S(2)}) %copy-start.1) | copy-done | bytes 1048600
  2.5 0.0 copy-start.2
  2.5 1.2 %copy-done.2 = bf16[2,512,512]{2,1,0:T(8,128)(2,1)S(1)} copy-done((bf16[2,512,512]{2,1,0:T(8,128)(2,1)S(1)}, bf16[2,512,512]{2,1,0:T(8,128)(2,1)}, u32[]{:S(2)}) %copy-start.2) | copy-done | bytes 1048600
  3.7 0.0 copy-start.3
  3.7 1.1 %copy-done.3 = f32[3,2,256,128]{3,2,1,0:T(8,128)S(1)} copy-done((f32[3,2,256,128]{3,2,1,0:T(8,128)S(1)}, f32[3,2,256,128]{3,2,1,0:T(8,128)}, u32[]{:S(2)}) %copy-start.3) | copy-done | bytes 786456
  4.8 75.0 %correlate.1 = f32[2,32,32,128]{3,2,1,0:T(8,128)S(1)} custom-call(f32[2,32,32,128]{3,2,1,0:T(8,128)S(1)} %bitcast.4, f32[2,32,32,128]{3,2,1,0:T(8,128)S(1)} %bitcast.5, bf16[2,512,512]{2,1,0:T(8,128)(2,1)S(1)} %copy-done.2, f32[3,2,256,128]{3,2,1,0:T(8,128)S(1)} %copy-done.3), custom_call_target="tpu_custom_call" | custom-call | tf_op jit(solution)/shard_map/correlate/pallas_call | solution.py:275
  79.8 1.0 %copy.7 = f32[2,32,1,4096]{3,2,1,0:T(1,128)} copy(f32[2,32,1,4096]{3,2,1,0:T(1,128)S(1)} %bitcast.3) | data formatting | bytes 2097152
Async XLA Ops:
  0.0 1.2 %copy-start = (f32[2,32,1,4096]{3,2,1,0:T(1,128)S(1)}, f32[2,32,1,4096]{3,2,1,0:T(1,128)}, u32[]{:S(2)}) copy-start(f32[2,32,1,4096]{3,2,1,0:T(1,128)} %param.4) | copy-start | bytes 3145732
  1.2 1.2 %copy-start.1 = (f32[2,32,1,4096]{3,2,1,0:T(1,128)S(1)}, f32[2,32,1,4096]{3,2,1,0:T(1,128)}, u32[]{:S(2)}) copy-start(f32[2,32,1,4096]{3,2,1,0:T(1,128)} %param.5) | copy-start | bytes 3145732
  2.5 1.2 %copy-start.2 = (bf16[2,512,512]{2,1,0:T(8,128)(2,1)S(1)}, bf16[2,512,512]{2,1,0:T(8,128)(2,1)}, u32[]{:S(2)}) copy-start(bf16[2,512,512]{2,1,0:T(8,128)(2,1)} %constant.4.clone.dft_hbm) | copy-start | bytes 3145732
  3.7 1.1 %copy-start.3 = (f32[3,2,256,128]{3,2,1,0:T(8,128)S(1)}, f32[3,2,256,128]{3,2,1,0:T(8,128)}, u32[]{:S(2)}) copy-start(f32[3,2,256,128]{3,2,1,0:T(8,128)} %constant.5.clone.tw_hbm) | copy-start | bytes 2359300
where the time goes:
time: 81 us; the launch traced here: 80.8 us
  Pallas kernels  75 us (93%)
  local copies, waits for them, and re-layouts  5.78 us (7%)
    pallas_call x1, Pallas kernels, on_device(): pl.pallas_call(functools.partial(body, n_energy, side), out_shape=jax.Sha...  75 us
    unnamed x9, local copies, waits for them, and re-layouts  5.78 us

commit v1 on v0

v1 whole, which is shorter than its diff:
```python
import functools
import math

import jax
import jax.numpy as jnp
import ml_dtypes
import numpy as np
from jax import lax
from jax.experimental import pallas as pl
from jax.experimental.pallas import tpu as pltpu
from jax.sharding import PartitionSpec as P

MESH = pl.DeviceIdType.MESH
BF = jnp.bfloat16
F32 = jnp.float32


def tables(energies, lanes):
    length = 2 * energies
    quarter = length // 4
    n = np.arange(quarter)
    angle = 2.0 * np.pi * (np.outer(n, n) % quarter) / quarter
    cos, sin = np.cos(angle), np.sin(angle)
    full = np.block([[cos, sin], [-sin, cos]]).astype(np.float32)
    high = full.astype(ml_dtypes.bfloat16)
    low = (full - high.astype(np.float32)).astype(ml_dtypes.bfloat16)
    rows = []
    for q in (1, 2, 3):
        turn = 2.0 * np.pi * ((n * q) % length) / length
        rows.append(np.stack([np.cos(turn), -np.sin(turn)]))
    twiddle = np.stack(rows).astype(np.float32)
    twiddle = np.ascontiguousarray(np.broadcast_to(twiddle[..., None], twiddle.shape + (lanes,)))
    return np.stack([high, low]), twiddle


def split(x):
    high = x.astype(BF)
    return high, (x - high.astype(F32)).astype(BF)


def body(
    n_energy, side, lesser, greater, dft_hbm, tw_hbm, out,
    g_in, stage, turned, mirror_out, l_buf, g_buf, p_buf, held, dft, tw, y_hi, y_lo, spec, v_hi, v_lo, back,
    in_sem, own_sem, l_send, g_send, p_send, l_recv, g_recv, p_recv, r_recv, f_send,
):
    e = lax.axis_index("energy")
    t = lax.axis_index("tile")
    t2 = (t % side) * side + t // side
    off_diagonal = t2 != t
    local = g_in.shape[1]
    energies = n_energy * local
    half = energies // 2

    load_g = pltpu.make_async_copy(greater, g_in, in_sem.at[0])
    load_g.start()
    load_dft = pltpu.make_async_copy(dft_hbm, dft, in_sem.at[1])
    load_tw = pltpu.make_async_copy(tw_hbm, tw, in_sem.at[2])

    mirror = lambda k: (k % side) * side + k // side
    n_tile = side * side
    group = n_energy // 2
    base = (e // group) * group
    across = lambda k: (k + n_tile // 2) % n_tile
    crosses = lambda k: mirror(k) // (n_tile // 2) != k // (n_tile // 2)
    cross = crosses(t)
    relay = across(t)
    hands = crosses(relay)
    final = mirror(relay)
    last = across(t2)
    plain = jnp.logical_and(off_diagonal, jnp.logical_not(cross))

    barrier = pltpu.get_barrier_semaphore()

    def greet(to, tile):
        pl.semaphore_signal(barrier, inc=1, device_id=(to, tile), device_id_type=MESH)

    @pl.loop(1, n_energy)
    def _(m):
        greet((e + m) % n_energy, t)

    @pl.when(plain)
    def _():
        @pl.loop(0, n_energy)
        def _(m):
            greet((e + m) % n_energy, t2)

    @pl.when(cross)
    def _():
        greet(e, relay)

        @pl.loop(0, group)
        def _(m):
            greet((base + group + m) % n_energy, t2)
            greet(base + m, last)

    @pl.when(hands)
    def _():
        greet(e, relay)

        @pl.loop(0, group)
        def _(m):
            greet(base + m, final)

    def l_copy(h, to, frm):
        return pltpu.make_async_remote_copy(
            src_ref=lesser.at[:, :, h * n_energy + to],
            dst_ref=l_buf.at[h, :, pl.ds(pl.multiple_of(frm * local, local), local)],
            send_sem=l_send.at[h, to],
            recv_sem=l_recv.at[h, frm],
            device_id=(to, t),
            device_id_type=MESH,
        )

    def g_copy(h, to, frm):
        return pltpu.make_async_remote_copy(
            src_ref=mirror_out.at[:, :, h * n_energy + to],
            dst_ref=g_buf.at[h, :, pl.ds(pl.multiple_of(frm * local, local), local)],
            send_sem=g_send.at[h, to],
            recv_sem=g_recv.at[h, frm],
            device_id=(to, t2),
            device_id_type=MESH,
        )

    def first_leg(h, m):
        to = base + m
        return pltpu.make_async_remote_copy(
            src_ref=mirror_out.at[:, :, h * n_energy + to],
            dst_ref=held.at[h, m],
            send_sem=g_send.at[h, to],
            recv_sem=r_recv.at[h, m],
            device_id=(e, relay),
            device_id_type=MESH,
        )

    def second_leg(h, m):
        return pltpu.make_async_remote_copy(
            src_ref=held.at[h, m],
            dst_ref=g_buf.at[h, :, pl.ds(pl.multiple_of(e * local, local), local)],
            send_sem=f_send.at[h, m],
            recv_sem=g_recv.at[h, e],
            device_id=(base + m, final),
            device_id_type=MESH,
        )

    def p_copy(h, to, frm):
        return pltpu.make_async_remote_copy(
            src_ref=p_buf.at[h, :, pl.ds(pl.multiple_of(to * local, local), local)],
            dst_ref=out.at[:, :, h * n_energy + frm],
            send_sem=p_send.at[h, to],
            recv_sem=p_recv.at[h, frm],
            device_id=(to, t),
            device_id_type=MESH,
        )

    def l_own(h):
        return pltpu.make_async_copy(
            lesser.at[:, :, h * n_energy + e], l_buf.at[h, :, pl.ds(pl.multiple_of(e * local, local), local)], l_recv.at[h, e]
        )

    def g_own(h):
        return pltpu.make_async_copy(
            mirror_out.at[:, :, h * n_energy + e], g_buf.at[h, :, pl.ds(pl.multiple_of(e * local, local), local)], g_recv.at[h, e]
        )

    def p_own(h):
        return pltpu.make_async_copy(
            p_buf.at[h, :, pl.ds(pl.multiple_of(e * local, local), local)], out.at[:, :, h * n_energy + e], p_recv.at[h, e]
        )

    def send_l(h):
        @pl.loop(1, n_energy)
        def _(m):
            l_copy(h, (e + m) % n_energy, e).start()

        l_own(h).start()

    def send_g(h):
        @pl.when(cross)
        def _():
            @pl.loop(0, group)
            def _(m):
                k = (e + m) % group
                first_leg(h, k).start()
                g_copy(h, (base + group) % n_energy + k, e).start()

        @pl.when(jnp.logical_not(cross))
        def _():
            @pl.loop(1, n_energy)
            def _(m):
                g_copy(h, (e + m) % n_energy, e).start()

            @pl.when(off_diagonal)
            def _():
                g_copy(h, e, e).start()

            @pl.when(jnp.logical_not(off_diagonal))
            def _():
                g_own(h).start()

    def hand_on(h):
        @pl.when(hands)
        def _():
            @pl.loop(0, group)
            def _(m):
                k = (e + m) % group
                first_leg(h, k).wait_recv()
                second_leg(h, k).start()

    load_dft.start()
    load_tw.start()
    load_g.wait()

    low_lanes = lax.broadcasted_iota(jnp.int32, (32, 128), 1) < 64

    groups = stage.shape[0]

    @pl.loop(0, 2 * local // (4 * groups))
    def _(step):
        for k in range(groups):
            item = step * groups + k
            p = item // (local // 4)
            e0 = (item % (local // 4)) * 4
            for q in range(2):
                one = g_in[p, e0 + 2 * q]
                two = g_in[p, e0 + 2 * q + 1]
                stage[k, pl.ds(64 * q, 32, stride=2), :] = jnp.where(low_lanes, one, pltpu.roll(two, 64, 1))
                stage[k, pl.ds(64 * q + 1, 32, stride=2), :] = jnp.where(low_lanes, pltpu.roll(one, 64, 1), two)
        for k in range(groups):
            turned[k] = stage[k].T
        for k in range(groups):
            item = step * groups + k
            p = item // (local // 4)
            e0 = (item % (local // 4)) * 4
            for w in range(2):
                even = turned[k, pl.ds(64 * w, 32, stride=2), :]
                odd = turned[k, pl.ds(64 * w + 1, 32, stride=2), :]
                mirror_out[p, e0 + w] = jnp.where(low_lanes, even, pltpu.roll(odd, 64, 1))
                mirror_out[p, e0 + 2 + w] = jnp.where(low_lanes, pltpu.roll(even, 64, 1), odd)

    factor = 1.0 / (2 * energies * math.sqrt(energies))

    def put(column, re, im):
        hi, lo = split(re)
        y_hi[:half, column : column + 128] = hi
        y_lo[:half, column : column + 128] = lo
        hi, lo = split(im)
        y_hi[half:, column : column + 128] = hi
        y_lo[half:, column : column + 128] = lo

    def front(buf, h, base, sign):
        re0, re1 = buf[h, 0, :half], buf[h, 0, half:]
        im0, im1 = sign * buf[h, 1, :half], sign * buf[h, 1, half:]
        put(base, re0 + re1, im0 + im1)
        for q, re, im in (
            (1, re0 + im1, im0 - re1),
            (2, re0 - re1, im0 - im1),
            (3, re0 - im1, im0 + re1),
        ):
            c, s = tw[q - 1, 0], tw[q - 1, 1]
            put(base + 128 * q, re * c - im * s, re * s + im * c)

    def dots(rows, hi, lo, columns):
        dot = functools.partial(jnp.dot, preferred_element_type=F32)
        high, low = dft[0, rows], dft[1, rows]
        return dot(high, hi[:, columns]) + dot(high, lo[:, columns]) + dot(low, hi[:, columns])

    def wait_l(h):
        @pl.loop(1, n_energy)
        def _(m):
            l_copy(h, e, (e + n_energy - m) % n_energy).wait_recv()

        l_own(h).wait()

    def wait_g(h):
        @pl.loop(0, n_energy)
        def _(m):
            frm = (e + n_energy - m) % n_energy
            pltpu.make_async_copy(
                mirror_out.at[:, :, 0], g_buf.at[h, :, pl.ds(pl.multiple_of(frm * local, local), local)], g_recv.at[h, frm]
            ).wait()

    def compute_l(h):
        front(l_buf, h, 0, 1.0)
        for c in range(2):
            columns = slice(256 * c, 256 * c + 256)
            spec[:, columns] = dots(slice(None), y_hi, y_lo, columns)

    def compute_g(h):
        front(g_buf, h, 512, -1.0)
        for c in range(2, 4):
            columns = slice(256 * c, 256 * c + 256)
            spec[:, columns] = dots(slice(None), y_hi, y_lo, columns)
        for c in range(4):
            one, two = slice(128 * c, 128 * c + 128), slice(512 + 128 * c, 640 + 128 * c)
            ar, ai = spec[:half, one], spec[half:, one]
            br, bi = spec[:half, two], spec[half:, two]
            hi, lo = split(ar * br + ai * bi)
            v_hi[:half, one] = hi
            v_lo[:half, one] = lo
            hi, lo = split(ar * bi - ai * br)
            v_hi[half:, one] = hi
            v_lo[half:, one] = lo

    def finish(h, part):
        count = half // 2
        low, high = slice(count * part, count * part + count), slice(half + count * part, half + count * part + count)
        for c in range(2):
            columns = slice(256 * c, 256 * c + 256)
            back[low, columns] = dots(low, v_hi, v_lo, columns)
            back[high, columns] = dots(high, v_hi, v_lo, columns)
        terms = [(back[low, :128], back[high, :128])]
        for q in (1, 2, 3):
            re, im = back[low, 128 * q : 128 * q + 128], back[high, 128 * q : 128 * q + 128]
            c, s = tw[q - 1, 0, low], tw[q - 1, 1, low]
            terms.append((re * c - im * s, re * s + im * c))
        (r0, i0), (r1, i1), (r2, i2), (r3, i3) = terms
        p_buf[h, 0, low] = (i0 + i1 + i2 + i3) * -factor
        p_buf[h, 1, low] = (r0 + r1 + r2 + r3) * -factor
        p_buf[h, 0, high] = (i0 - r1 - i2 + r3) * -factor
        p_buf[h, 1, high] = (r0 + i1 - r2 - i3) * -factor

    def send_p(h, part):
        @pl.loop(0, n_energy // 2)
        def _(m):
            turn = (e + m) % (n_energy // 2)
            to = (turn // (n_energy // 4)) * group + part * (n_energy // 4) + turn % (n_energy // 4)

            @pl.when(to != e)
            def _():
                p_copy(h, to, e).start()

            @pl.when(to == e)
            def _():
                p_own(h).start()

    def drain_l(h):
        @pl.loop(1, n_energy)
        def _(m):
            l_copy(h, (e + m) % n_energy, e).wait_send()

    def drain_g(h):
        @pl.loop(1, n_energy)
        def _(m):
            g_copy(h, (e + m) % n_energy, e).wait_send()

        @pl.when(off_diagonal)
        def _():
            g_copy(h, e, e).wait_send()

        @pl.when(hands)
        def _():
            @pl.loop(0, group)
            def _(m):
                second_leg(h, m).wait_send()

    def drain_p(h):
        @pl.loop(1, n_energy)
        def _(m):
            to = (e + m) % n_energy
            p_copy(h, to, e).wait_send()
            p_copy(h, e, to).wait_recv()

        p_own(h).wait()

    signals = n_energy - 1 + jnp.where(plain, n_energy, 0)
    signals += jnp.where(cross, n_energy + 1, 0) + jnp.where(hands, group + 1, 0)
    pl.semaphore_wait(barrier, signals)

    send_g(0)
    send_l(0)
    send_g(1)
    send_l(1)
    hand_on(0)
    hand_on(1)
    load_dft.wait()
    load_tw.wait()

    @pl.loop(0, 2)
    def _(h):
        wait_l(h)
        compute_l(h)
        wait_g(h)
        compute_g(h)
        for part in range(2):
            finish(h, part)
            send_p(h, part)

    @pl.loop(0, 2)
    def _(h):
        drain_l(h)
        drain_g(h)
        drain_p(h)


def on_device(lesser, greater):
    n_energy = lax.axis_size("energy")
    side = math.isqrt(lax.axis_size("tile"))
    local, cells = lesser.shape[1], lesser.shape[3]
    rows = cells // 128
    energies = n_energy * local
    dft, twiddle = tables(energies, 128)
    any_space = pl.BlockSpec(memory_space=pltpu.HBM)
    half = energies // 2
    out = pl.pallas_call(
        functools.partial(body, n_energy, side),
        out_shape=jax.ShapeDtypeStruct((2, local, rows, 128), F32),
        in_specs=[any_space] * 4,
        out_specs=any_space,
        scratch_shapes=[
            pltpu.VMEM((2, local, rows, 128), F32),
            pltpu.VMEM((4, 128, 128), F32),
            pltpu.VMEM((4, 128, 128), F32),
            pltpu.VMEM((2, local, rows, 128), F32),
            pltpu.VMEM((2, 2, energies, 128), F32),
            pltpu.VMEM((2, 2, energies, 128), F32),
            pltpu.VMEM((2, 2, energies, 128), F32),
            pltpu.VMEM((2, n_energy // 2, 2, local, 128), F32),
            pltpu.VMEM((2, energies, energies), BF),
            pltpu.VMEM((3, 2, half, 128), F32),
            pltpu.VMEM((energies, 1024), BF),
            pltpu.VMEM((energies, 1024), BF),
            pltpu.VMEM((energies, 1024), F32),
            pltpu.VMEM((energies, 512), BF),
            pltpu.VMEM((energies, 512), BF),
            pltpu.VMEM((energies, 512), F32),
            pltpu.SemaphoreType.DMA((3,)),
            pltpu.SemaphoreType.DMA((2,)),
        ]
        + [pltpu.SemaphoreType.DMA((2, n_energy))] * 6
        + [pltpu.SemaphoreType.DMA((2, n_energy // 2))] * 2,
        compiler_params=pltpu.CompilerParams(
            collective_id=0, has_side_effects=True, vmem_limit_bytes=60 * 2**20
        ),
        name="correlate",
    )(
        lesser.reshape(2, local, rows, 128),
        greater.reshape(2, local, rows, 128),
        jnp.asarray(dft),
        jnp.asarray(twiddle),
    )
    return out.reshape(2, local, 1, cells)


def solution(mesh):
    return jax.shard_map(
        on_device,
        mesh=mesh,
        in_specs=(P(None, "energy", "tile", None), P(None, "energy", "tile", None)),
        out_specs=P(None, "energy", "tile", None),
        check_vma=False,
    )
```

time: 81 us -> 59 us (0.73)
  Pallas kernels: 75 us -> 55.8 us
  local copies, waits for them, and re-layouts: 5.78 us -> 2.26 us
    pallas_call x1, Pallas kernels: 75 us -> 55.8 us  [on_device(): pl.pallas_call(functools.partial(body, n_energy, side), out_shape=jax.Sha...]
    unnamed x9 -> x1, local copies, waits for them, and re-layouts: 5.78 us -> 2.26 us
where the time goes in v1:
time: 59 us; the launch traced here: 58 us
  Pallas kernels  55.8 us (95%)
  local copies, waits for them, and re-layouts  2.26 us (4%)
    pallas_call x1, Pallas kernels, on_device(): pl.pallas_call(functools.partial(body, n_energy, side), out_shape=jax.Sha...  55.8 us
    unnamed x1, local copies, waits for them, and re-layouts  2.26 us

profile of v1, /device:TPU:97, one launch (start us, length us, event | category | flops | bytes accessed | tf_op | source)
XLA Modules:
  0.0 58.0 jit_solution(211879257419114913)
XLA Ops:
  0.0 55.8 %correlate.1 = f32[2,32,32,128]{3,2,1,0:T(8,128)} custom-call(f32[2,32,32,128]{3,2,1,0:T(8,128)} %bitcast.4, f32[2,32,32,128]{3,2,1,0:T(8,128)} %bitcast.5, bf16[2,512,512]{2,1,0:T(8,128)(2,1)} %constant.4.clone.dft_hbm, f32[3,2,256,128]{3,2,1,0:T(8,128)} %constant.5.clone.tw_hbm), custom_call_target="tpu_custom_call" | custom-call | tf_op jit(solution)/shard_map/correlate/pallas_call | solution.py:404
  55.8 2.3 %copy.7 = f32[2,32,1,4096]{3,2,1,0:T(1,128)} copy(f32[2,32,1,4096]{3,2,1,0:T(1,128)} %bitcast.3) | data formatting | bytes 2097152

commit v2 on v1

--- a/solution.py
+++ b/solution.py
@@ -429,14 +429,14 @@
         + [pltpu.SemaphoreType.DMA((2, n_energy))] * 6
         + [pltpu.SemaphoreType.DMA((2, n_energy // 2))] * 2,
         compiler_params=pltpu.CompilerParams(
-            collective_id=0, has_side_effects=True, vmem_limit_bytes=60 * 2**20
+            collective_id=0, has_side_effects=True, vmem_limit_bytes=40 * 2**20
         ),
         name="correlate",
     )(
-        lesser.reshape(2, local, rows, 128),
-        greater.reshape(2, local, rows, 128),
-        jnp.asarray(dft),
-        jnp.asarray(twiddle),
+        pltpu.with_memory_space_constraint(lesser.reshape(2, local, rows, 128), pltpu.HBM),
+        pltpu.with_memory_space_constraint(greater.reshape(2, local, rows, 128), pltpu.HBM),
+        pltpu.with_memory_space_constraint(jnp.asarray(dft), pltpu.HBM),
+        pltpu.with_memory_space_constraint(jnp.asarray(twiddle), pltpu.HBM),
     )
     return out.reshape(2, local, 1, cells)
 

time: 59 us -> 57.5 us (0.975)
  local copies, waits for them, and re-layouts: 2.26 us -> 0.97 us
    unnamed x1, local copies, waits for them, and re-layouts: 2.26 us -> 0.97 us
where the time goes in v2:
time: 57.5 us; the launch traced here: 56.6 us
  Pallas kernels  55.7 us (97%)
  local copies, waits for them, and re-layouts  0.97 us (2%)
    pallas_call x1, Pallas kernels, on_device(): pl.pallas_call(functools.partial(body, n_energy, side), out_shape=jax.Sha...  55.7 us

profile of v2, /device:TPU:97, one launch (start us, length us, event | category | flops | bytes accessed | tf_op | source)
XLA Modules:
  0.0 56.6 jit_solution(4244219906979687144)
XLA Ops:
  0.0 55.7 %correlate.1 = f32[2,32,32,128]{3,2,1,0:T(8,128)S(1)} custom-call(f32[2,32,32,128]{3,2,1,0:T(8,128)} %bitcast.4, f32[2,32,32,128]{3,2,1,0:T(8,128)} %bitcast.5, bf16[2,512,512]{2,1,0:T(8,128)(2,1)} %constant.4.clone.dft_hbm, f32[3,2,256,128]{3,2,1,0:T(8,128)} %constant.5.clone.tw_hbm), custom_call_target="tpu_custom_call" | custom-call | tf_op jit(solution)/shard_map/correlate/pallas_call | solution.py:404
  55.7 1.0 %copy.7 = f32[2,32,1,4096]{3,2,1,0:T(1,128)} copy(f32[2,32,1,4096]{3,2,1,0:T(1,128)S(1)} %bitcast.3) | data formatting | bytes 2097152

commit v3 on v2

--- a/solution.py
+++ b/solution.py
@@ -33,6 +33,18 @@
     return np.stack([high, low]), twiddle
 
 
+HALF, ROUND = 1, 2
+KINDS = tuple((k, HALF) for k in (2, 3, 6, 7, 8, 9, 12, 13)) + tuple((k, ROUND) for k in (1, 4, 11, 14))
+ROUND_BY = ((1, 6), (4, 7), (11, 8), (14, 9))
+
+
+def pick(key, table):
+    value = jnp.int32(0)
+    for k, v in table:
+        value = jnp.where(key == k, jnp.int32(v), value)
+    return value
+
+
 def split(x):
     high = x.astype(BF)
     return high, (x - high.astype(F32)).astype(BF)
@@ -60,14 +72,25 @@
     n_tile = side * side
     group = n_energy // 2
     base = (e // group) * group
-    across = lambda k: (k + n_tile // 2) % n_tile
-    crosses = lambda k: mirror(k) // (n_tile // 2) != k // (n_tile // 2)
-    cross = crosses(t)
-    relay = across(t)
-    hands = crosses(relay)
-    final = mirror(relay)
-    last = across(t2)
-    plain = jnp.logical_and(off_diagonal, jnp.logical_not(cross))
+    other = (e + group) % n_energy
+    across = (t + n_tile // 2) % n_tile
+    kind = pick(t, KINDS)
+    relay = jnp.where(kind == ROUND, pick(t, ROUND_BY), across)
+    round_from = pick(t, [(b, a) for a, b in ROUND_BY])
+    source = jnp.where(round_from > 0, round_from, across)
+    hands = pick(source, KINDS)
+    hands = jnp.where(jnp.logical_and(hands == ROUND, round_from == 0), 0, hands)
+    final = mirror(source)
+    gets = pick(t2, KINDS)
+    last = jnp.where(gets == ROUND, pick(t2, ROUND_BY), (t2 + n_tile // 2) % n_tile)
+
+    def by_relay(how, frm, to):
+        same = to // group == frm // group
+        return jnp.logical_or(
+            jnp.logical_and(how == HALF, same), jnp.logical_and(how == ROUND, (to + frm) % 4 == 0)
+        )
+
+    fourth = lambda m: 4 * m + (n_energy - e) % 4
 
     barrier = pltpu.get_barrier_semaphore()
 
@@ -78,28 +101,34 @@
     def _(m):
         greet((e + m) % n_energy, t)
 
-    @pl.when(plain)
+    @pl.when(off_diagonal)
     def _():
         @pl.loop(0, n_energy)
         def _(m):
             greet((e + m) % n_energy, t2)
 
-    @pl.when(cross)
-    def _():
-        greet(e, relay)
-
-        @pl.loop(0, group)
-        def _(m):
-            greet((base + group + m) % n_energy, t2)
-            greet(base + m, last)
-
-    @pl.when(hands)
-    def _():
-        greet(e, relay)
-
-        @pl.loop(0, group)
-        def _(m):
-            greet(base + m, final)
+    def greet_relay(how, tile):
+        @pl.when(how > 0)
+        def _():
+            greet(e, tile)
+
+    def greet_group(how, tile):
+        @pl.when(how == HALF)
+        def _():
+            @pl.loop(0, group)
+            def _(m):
+                greet(base + m, tile)
+
+        @pl.when(how == ROUND)
+        def _():
+            @pl.loop(0, n_energy // 4)
+            def _(m):
+                greet(fourth(m), tile)
+
+    greet_relay(kind, relay)
+    greet_relay(hands, source)
+    greet_group(hands, final)
+    greet_group(gets, last)
 
     def l_copy(h, to, frm):
         return pltpu.make_async_remote_copy(
@@ -121,26 +150,31 @@
             device_id_type=MESH,
         )
 
-    def first_leg(h, m):
-        to = base + m
+    def first_leg(h, to):
         return pltpu.make_async_remote_copy(
             src_ref=mirror_out.at[:, :, h * n_energy + to],
-            dst_ref=held.at[h, m],
+            dst_ref=held.at[h, jnp.where(to // group == e // group, 0, 1), to % group],
             send_sem=g_send.at[h, to],
-            recv_sem=r_recv.at[h, m],
-            device_id=(e, relay),
+            recv_sem=r_recv.at[h, jnp.where(to // group == e // group, 0, 1), to % group],
+            device_id=(jnp.where(kind == ROUND, e, (to // group) * group + e % group), relay),
             device_id_type=MESH,
         )
 
-    def second_leg(h, m):
+    def second_leg(h, k, m):
+        frm = e if k == 0 else jnp.where(hands == ROUND, e, other)
+        to = base + m if k == 0 else jnp.where(hands == ROUND, (base + group) % n_energy, base) + m
         return pltpu.make_async_remote_copy(
-            src_ref=held.at[h, m],
-            dst_ref=g_buf.at[h, :, pl.ds(pl.multiple_of(e * local, local), local)],
-            send_sem=f_send.at[h, m],
-            recv_sem=g_recv.at[h, e],
-            device_id=(base + m, final),
+            src_ref=held.at[h, k, m],
+            dst_ref=g_buf.at[h, :, pl.ds(pl.multiple_of(frm * local, local), local)],
+            send_sem=f_send.at[h, k, m],
+            recv_sem=g_recv.at[h, frm],
+            device_id=(to, final),
             device_id_type=MESH,
         )
+
+    def handed(k, m):
+        quarter = jnp.logical_and(hands == ROUND, (m + e) % 4 == 0)
+        return jnp.logical_or(hands == HALF, quarter) if k == 0 else quarter
 
     def p_copy(h, to, frm):
         return pltpu.make_async_remote_copy(
@@ -174,37 +208,44 @@
 
         l_own(h).start()
 
-    def send_g(h):
-        @pl.when(cross)
+    def send_legs(h):
+        @pl.when(kind == ROUND)
+        def _():
+            @pl.loop(0, n_energy // 4)
+            def _(m):
+                first_leg(h, fourth(m)).start()
+
+        @pl.when(kind == HALF)
         def _():
             @pl.loop(0, group)
             def _(m):
-                k = (e + m) % group
-                first_leg(h, k).start()
-                g_copy(h, (base + group) % n_energy + k, e).start()
-
-        @pl.when(jnp.logical_not(cross))
-        def _():
-            @pl.loop(1, n_energy)
-            def _(m):
-                g_copy(h, (e + m) % n_energy, e).start()
-
-            @pl.when(off_diagonal)
-            def _():
-                g_copy(h, e, e).start()
-
-            @pl.when(jnp.logical_not(off_diagonal))
-            def _():
-                g_own(h).start()
+                first_leg(h, base + (e + m) % group).start()
+
+    def send_g(h):
+        @pl.loop(0, group)
+        def _(m):
+            for start in (base, (base + group) % n_energy):
+                to = start + (e + m) % group
+                own = jnp.logical_and(to == e, jnp.logical_not(off_diagonal))
+
+                @pl.when(jnp.logical_not(jnp.logical_or(by_relay(kind, e, to), own)))
+                def _():
+                    g_copy(h, to, e).start()
+
+        @pl.when(jnp.logical_not(off_diagonal))
+        def _():
+            g_own(h).start()
 
     def hand_on(h):
-        @pl.when(hands)
-        def _():
-            @pl.loop(0, group)
-            def _(m):
-                k = (e + m) % group
-                first_leg(h, k).wait_recv()
-                second_leg(h, k).start()
+        @pl.loop(0, group)
+        def _(step):
+            m = (e + step) % group
+            for k in range(2):
+
+                @pl.when(handed(k, m))
+                def _():
+                    pltpu.make_async_copy(mirror_out.at[:, :, 0], held.at[h, k, m], r_recv.at[h, k, m]).wait()
+                    second_leg(h, k, m).start()
 
     load_dft.start()
     load_tw.start()
@@ -302,28 +343,38 @@
             v_lo[half:, one] = lo
 
     def finish(h, part):
+        blocks = [slice(local * (2 * k + part), local * (2 * k + part) + local) for k in range(n_energy // 4)]
+        later = [slice(half + b.start, half + b.stop) for b in blocks]
+        take = lambda ref, index, rows: jnp.concatenate([ref[(*index, r)] for r in rows])
         count = half // 2
-        low, high = slice(count * part, count * part + count), slice(half + count * part, half + count * part + count)
         for c in range(2):
             columns = slice(256 * c, 256 * c + 256)
-            back[low, columns] = dots(low, v_hi, v_lo, columns)
-            back[high, columns] = dots(high, v_hi, v_lo, columns)
-        terms = [(back[low, :128], back[high, :128])]
+            for rows, to in ((blocks, slice(0, count)), (later, slice(count, half))):
+                dot = functools.partial(jnp.dot, preferred_element_type=F32)
+                high, low = take(dft, (0,), rows), take(dft, (1,), rows)
+                back[to, columns] = (
+                    dot(high, v_hi[:, columns]) + dot(high, v_lo[:, columns]) + dot(low, v_hi[:, columns])
+                )
+        terms = [(back[:count, :128], back[count:half, :128])]
         for q in (1, 2, 3):
-            re, im = back[low, 128 * q : 128 * q + 128], back[high, 128 * q : 128 * q + 128]
-            c, s = tw[q - 1, 0, low], tw[q - 1, 1, low]
+            re, im = back[:count, 128 * q : 128 * q + 128], back[count:half, 128 * q : 128 * q + 128]
+            c, s = take(tw, (q - 1, 0), blocks), take(tw, (q - 1, 1), blocks)
             terms.append((re * c - im * s, re * s + im * c))
         (r0, i0), (r1, i1), (r2, i2), (r3, i3) = terms
-        p_buf[h, 0, low] = (i0 + i1 + i2 + i3) * -factor
-        p_buf[h, 1, low] = (r0 + r1 + r2 + r3) * -factor
-        p_buf[h, 0, high] = (i0 - r1 - i2 + r3) * -factor
-        p_buf[h, 1, high] = (r0 + i1 - r2 - i3) * -factor
+        values = (
+            (0, blocks, i0 + i1 + i2 + i3),
+            (1, blocks, r0 + r1 + r2 + r3),
+            (0, later, i0 - r1 - i2 + r3),
+            (1, later, r0 + i1 - r2 - i3),
+        )
+        for p, rows, value in values:
+            for k, r in enumerate(rows):
+                p_buf[h, p, r] = value[local * k : local * k + local] * -factor
 
     def send_p(h, part):
-        @pl.loop(0, n_energy // 2)
-        def _(m):
-            turn = (e + m) % (n_energy // 2)
-            to = (turn // (n_energy // 4)) * group + part * (n_energy // 4) + turn % (n_energy // 4)
+        @pl.loop(0, group)
+        def _(m):
+            to = 2 * ((e // 2 + m) % group) + part
 
             @pl.when(to != e)
             def _():
@@ -347,11 +398,13 @@
         def _():
             g_copy(h, e, e).wait_send()
 
-        @pl.when(hands)
-        def _():
-            @pl.loop(0, group)
-            def _(m):
-                second_leg(h, m).wait_send()
+        @pl.loop(0, group)
+        def _(m):
+            for k in range(2):
+
+                @pl.when(handed(k, m))
+                def _():
+                    second_leg(h, k, m).wait_send()
 
     def drain_p(h):
         @pl.loop(1, n_energy)
@@ -362,16 +415,18 @@
 
         p_own(h).wait()
 
-    signals = n_energy - 1 + jnp.where(plain, n_energy, 0)
-    signals += jnp.where(cross, n_energy + 1, 0) + jnp.where(hands, group + 1, 0)
+    signals = n_energy - 1 + jnp.where(off_diagonal, n_energy, 0)
+    for how in (kind, hands):
+        signals += jnp.where(how > 0, 1, 0)
+    for how in (hands, gets):
+        signals += jnp.where(how == HALF, group, 0) + jnp.where(how == ROUND, n_energy // 4, 0)
     pl.semaphore_wait(barrier, signals)
 
-    send_g(0)
-    send_l(0)
-    send_g(1)
-    send_l(1)
-    hand_on(0)
-    hand_on(1)
+    for h in range(2):
+        send_legs(h)
+        send_g(h)
+        send_l(h)
+        hand_on(h)
     load_dft.wait()
     load_tw.wait()
 
@@ -414,7 +469,7 @@
             pltpu.VMEM((2, 2, energies, 128), F32),
             pltpu.VMEM((2, 2, energies, 128), F32),
             pltpu.VMEM((2, 2, energies, 128), F32),
-            pltpu.VMEM((2, n_energy // 2, 2, local, 128), F32),
+            pltpu.VMEM((2, 2, n_energy // 2, 2, local, 128), F32),
             pltpu.VMEM((2, energies, energies), BF),
             pltpu.VMEM((3, 2, half, 128), F32),
             pltpu.VMEM((energies, 1024), BF),
@@ -427,7 +482,7 @@
             pltpu.SemaphoreType.DMA((2,)),
         ]
         + [pltpu.SemaphoreType.DMA((2, n_energy))] * 6
-        + [pltpu.SemaphoreType.DMA((2, n_energy // 2))] * 2,
+        + [pltpu.SemaphoreType.DMA((2, 2, n_energy // 2))] * 2,
         compiler_params=pltpu.CompilerParams(
             collective_id=0, has_side_effects=True, vmem_limit_bytes=40 * 2**20
         ),

time: 57.5 us -> 56.2 us (0.977)
  the two profiles are of different devices: /device:TPU:97 before, /device:TPU:65 now
where the time goes in v3:
time: 56.2 us; the launch traced here: 56.1 us
  Pallas kernels  55.1 us (98%)
  local copies, waits for them, and re-layouts  0.97 us (2%)
    pallas_call x1, Pallas kernels, on_device(): pl.pallas_call(functools.partial(body, n_energy, side), out_shape=jax.Sha...  55.1 us

profile of v3, /device:TPU:65, one launch (start us, length us, event | category | flops | bytes accessed | tf_op | source)
XLA Modules:
  0.0 56.1 jit_solution(8225911740712574531)
XLA Ops:
  0.0 55.1 %correlate.1 = f32[2,32,32,128]{3,2,1,0:T(8,128)S(1)} custom-call(f32[2,32,32,128]{3,2,1,0:T(8,128)} %bitcast.4, f32[2,32,32,128]{3,2,1,0:T(8,128)} %bitcast.5, bf16[2,512,512]{2,1,0:T(8,128)(2,1)} %constant.4.clone.dft_hbm, f32[3,2,256,128]{3,2,1,0:T(8,128)} %constant.5.clone.tw_hbm), custom_call_target="tpu_custom_call" | custom-call | tf_op jit(solution)/shard_map/correlate/pallas_call | solution.py:459
  55.1 1.0 %copy.7 = f32[2,32,1,4096]{3,2,1,0:T(1,128)} copy(f32[2,32,1,4096]{3,2,1,0:T(1,128)S(1)} %bitcast.3) | data formatting | bytes 2097152

commit v4 on v3

--- a/solution.py
+++ b/solution.py
@@ -35,7 +35,7 @@
 
 HALF, ROUND = 1, 2
 KINDS = tuple((k, HALF) for k in (2, 3, 6, 7, 8, 9, 12, 13)) + tuple((k, ROUND) for k in (1, 4, 11, 14))
-ROUND_BY = ((1, 6), (4, 7), (11, 8), (14, 9))
+ROUND_BY = ((1, 7), (4, 6), (11, 9), (14, 8))
 
 
 def pick(key, table):
@@ -105,7 +105,11 @@
     def _():
         @pl.loop(0, n_energy)
         def _(m):
-            greet((e + m) % n_energy, t2)
+            to = (e + m) % n_energy
+
+            @pl.when(jnp.logical_not(by_relay(kind, e, to)))
+            def _():
+                greet(to, t2)
 
     def greet_relay(how, tile):
         @pl.when(how > 0)
@@ -416,6 +420,7 @@
         p_own(h).wait()
 
     signals = n_energy - 1 + jnp.where(off_diagonal, n_energy, 0)
+    signals -= jnp.where(kind == HALF, group, 0) + jnp.where(kind == ROUND, n_energy // 4, 0)
     for how in (kind, hands):
         signals += jnp.where(how > 0, 1, 0)
     for how in (hands, gets):

time: 56.2 us -> 54.4 us (0.968)
  the two profiles are of different devices: /device:TPU:65 before, /device:TPU:97 now
where the time goes in v4:
time: 54.4 us; the launch traced here: 53.5 us
  Pallas kernels  52.5 us (97%)
  local copies, waits for them, and re-layouts  0.97 us (2%)
    pallas_call x1, Pallas kernels, on_device(): pl.pallas_call(functools.partial(body, n_energy, side), out_shape=jax.Sha...  52.5 us

profile of v4, /device:TPU:97, one launch (start us, length us, event | category | flops | bytes accessed | tf_op | source)
XLA Modules:
  0.0 53.5 jit_solution(15044043277269048680)
XLA Ops:
  0.0 52.5 %correlate.1 = f32[2,32,32,128]{3,2,1,0:T(8,128)S(1)} custom-call(f32[2,32,32,128]{3,2,1,0:T(8,128)} %bitcast.4, f32[2,32,32,128]{3,2,1,0:T(8,128)} %bitcast.5, bf16[2,512,512]{2,1,0:T(8,128)(2,1)} %constant.4.clone.dft_hbm, f32[3,2,256,128]{3,2,1,0:T(8,128)} %constant.5.clone.tw_hbm), custom_call_target="tpu_custom_call" | custom-call | tf_op jit(solution)/shard_map/correlate/pallas_call | solution.py:464
  52.5 1.0 %copy.7 = f32[2,32,1,4096]{3,2,1,0:T(1,128)} copy(f32[2,32,1,4096]{3,2,1,0:T(1,128)S(1)} %bitcast.3) | data formatting | bytes 2097152

commit v5 on v4

--- a/solution.py
+++ b/solution.py
@@ -431,19 +431,27 @@
         send_legs(h)
         send_g(h)
         send_l(h)
-        hand_on(h)
+        if h == 0:
+            hand_on(h)
     load_dft.wait()
     load_tw.wait()
 
-    @pl.loop(0, 2)
-    def _(h):
+    def spectrum(h):
         wait_l(h)
         compute_l(h)
+
+    def rest(h):
         wait_g(h)
         compute_g(h)
         for part in range(2):
             finish(h, part)
             send_p(h, part)
+
+    spectrum(0)
+    hand_on(1)
+    rest(0)
+    spectrum(1)
+    rest(1)
 
     @pl.loop(0, 2)
     def _(h):

time: 54.4 us -> 53.8 us (0.989); the launches traced: 53.5 us -> 53.7 us
  no operation moved by 1% of the time
where the time goes in v5:
time: 53.8 us; the launch traced here: 53.7 us
  Pallas kernels  52.7 us (98%)
  local copies, waits for them, and re-layouts  0.97 us (2%)
    pallas_call x1, Pallas kernels, on_device(): pl.pallas_call(functools.partial(body, n_energy, side), out_shape=jax.Sha...  52.7 us

profile of v5, /device:TPU:97, one launch (start us, length us, event | category | flops | bytes accessed | tf_op | source)
XLA Modules:
  0.0 53.7 jit_solution(4320605148773519890)
XLA Ops:
  0.0 52.7 %correlate.1 = f32[2,32,32,128]{3,2,1,0:T(8,128)S(1)} custom-call(f32[2,32,32,128]{3,2,1,0:T(8,128)} %bitcast.4, f32[2,32,32,128]{3,2,1,0:T(8,128)} %bitcast.5, bf16[2,512,512]{2,1,0:T(8,128)(2,1)} %constant.4.clone.dft_hbm, f32[3,2,256,128]{3,2,1,0:T(8,128)} %constant.5.clone.tw_hbm), custom_call_target="tpu_custom_call" | custom-call | tf_op jit(solution)/shard_map/correlate/pallas_call | solution.py:472
  52.7 1.0 %copy.7 = f32[2,32,1,4096]{3,2,1,0:T(1,128)} copy(f32[2,32,1,4096]{3,2,1,0:T(1,128)S(1)} %bitcast.3) | data formatting | bytes 2097152

commit v6 on v5

--- a/solution.py
+++ b/solution.py
@@ -427,12 +427,12 @@
         signals += jnp.where(how == HALF, group, 0) + jnp.where(how == ROUND, n_energy // 4, 0)
     pl.semaphore_wait(barrier, signals)
 
-    for h in range(2):
-        send_legs(h)
-        send_g(h)
-        send_l(h)
-        if h == 0:
-            hand_on(h)
+    send_legs(0)
+    send_g(0)
+    send_l(0)
+    hand_on(0)
+    send_legs(1)
+    send_g(1)
     load_dft.wait()
     load_tw.wait()
 
@@ -449,6 +449,7 @@
 
     spectrum(0)
     hand_on(1)
+    send_l(1)
     rest(0)
     spectrum(1)
     rest(1)

time: 53.8 us -> 58.5 us (1.087)
  Pallas kernels: 52.7 us -> 57.2 us
    pallas_call x1, Pallas kernels: 52.7 us -> 57.2 us  [on_device(): pl.pallas_call(functools.partial(body, n_energy, side), out_shape=jax.Sha...]
where the time goes in v6:
time: 58.5 us; the launch traced here: 58.2 us
  Pallas kernels  57.2 us (98%)
  local copies, waits for them, and re-layouts  0.97 us (2%)
    pallas_call x1, Pallas kernels, on_device(): pl.pallas_call(functools.partial(body, n_energy, side), out_shape=jax.Sha...  57.2 us

profile of v6, /device:TPU:97, one launch (start us, length us, event | category | flops | bytes accessed | tf_op | source)
XLA Modules:
  0.0 58.2 jit_solution(11562156987751808308)
XLA Ops:
  0.0 57.2 %correlate.1 = f32[2,32,32,128]{3,2,1,0:T(8,128)S(1)} custom-call(f32[2,32,32,128]{3,2,1,0:T(8,128)} %bitcast.4, f32[2,32,32,128]{3,2,1,0:T(8,128)} %bitcast.5, bf16[2,512,512]{2,1,0:T(8,128)(2,1)} %constant.4.clone.dft_hbm, f32[3,2,256,128]{3,2,1,0:T(8,128)} %constant.5.clone.tw_hbm), custom_call_target="tpu_custom_call" | custom-call | tf_op jit(solution)/shard_map/correlate/pallas_call | solution.py:473
  57.2 1.0 %copy.7 = f32[2,32,1,4096]{3,2,1,0:T(1,128)} copy(f32[2,32,1,4096]{3,2,1,0:T(1,128)S(1)} %bitcast.3) | data formatting | bytes 2097152
